TPU v7x, 512 devices: a whole 4x4x16 slice. The times are simulated.
512 devices in a mesh: row: 16 (over z), col: 8 (over x, y_lo), rep: 4 (over y_hi, core).
Axes of the slice: x: 4, y: 4 (y_hi: 2, y_lo: 2; y = y_hi * 2 + y_lo), z: 16, core: 2. Of those that a mesh axis runs over, the one named last changes fastest.
Arguments:
- density: bfloat16 [8192, 8192], P(('row', 'rep'), 'col'), as said below
- reach: int32 [64], replicated, may hold values from 8 to 32
- slab_start: int32 [1], replicated, may hold values from 0 to 4096
Outputs:
- purified: float32 [4096, 8192], P('row', ('col', 'rep'))
Inputs may be any that keep to these rules, and one draw needn't show every extreme that they name: density is exactly symmetric.
All inputs are finite; a program needn't handle non-finite values.
Results may differ from a plain program's by a relative error of at most 0.0018.
Values may be sent and summed in bfloat16 or wider, within the bound.
A program may use at most 64 MiB of HBM per device.

v0:
```python
import jax
import jax.numpy as jnp
from jax import lax
from jax.sharding import PartitionSpec as P

SLAB_DEV = 256


def from_behind(value, axis, steps):
    count = lax.axis_size(axis)
    pairs = [(source, (source + steps) % count) for source in range(count)]
    return lax.ppermute(value, axis, pairs)


def cycle_product(left_panel, right_panel, left_dim, row_pos, row_count):
    block_size = right_panel.shape[0]
    slab_count = left_panel.shape[1 - left_dim]
    contract = (((left_dim,), (0,)), ((), ()))

    def partial_value(current, offset):
        source = (row_pos - offset) % row_count
        left_rows = lax.dynamic_slice_in_dim(left_panel, source * block_size, block_size, left_dim)
        return lax.dot_general(left_rows, current, contract, preferred_element_type=jnp.float32)

    def advance(state_pair, offset):
        current, running = state_pair
        running = running + partial_value(current, offset)
        shifted = from_behind(current, "row", 1)
        return ((shifted, running), current)

    initial = jnp.zeros((slab_count, right_panel.shape[1]), jnp.float32)
    (final_panel, running), passed = lax.scan(
        advance, (right_panel, initial), jnp.arange(row_count - 1)
    )
    running = running + partial_value(final_panel, row_count - 1)
    panels_kept = jnp.concatenate([passed, final_panel[None]], axis=0)
    return (running, panels_kept)


def local(density, reach, slab_start):
    row_pos = lax.axis_index("row")
    rep_pos = lax.axis_index("rep")
    col_pos = lax.axis_index("col")
    row_count = lax.axis_size("row")
    rep_count = lax.axis_size("rep")
    block_size = density.shape[0]
    tile_cols = density.shape[1]
    tile_blocks = tile_cols // block_size
    block_count = reach.shape[0]
    own_block = row_pos * rep_count + rep_pos
    blocks = jnp.arange(block_count)
    own_reach = jnp.sum(jnp.where(blocks == own_block, reach, 0))
    column_blocks = col_pos * tile_blocks + jnp.arange(tile_blocks)
    column_reach = lax.dynamic_slice_in_dim(reach, col_pos * tile_blocks, tile_blocks, 0)
    spread = jnp.abs(column_blocks - own_block)
    spread = jnp.minimum(spread, block_count - spread)
    kept_mask = spread <= jnp.minimum(column_reach, own_reach)
    shaped = density.reshape(block_size, tile_blocks, block_size)
    masked = jnp.where(kept_mask[None, :, None], shaped, jnp.zeros_like(shaped)).reshape(
        block_size, tile_cols
    )
    full_rows = lax.all_gather(masked, "col", axis=1, tiled=True)
    slab_cols = SLAB_DEV * row_count
    slab_part = lax.dynamic_slice_in_dim(full_rows, slab_start[0], slab_cols, 1)
    left_first = lax.all_to_all(slab_part, "row", split_axis=1, concat_axis=0, tiled=True)
    square_part, kept_panels = cycle_product(left_first, masked, 0, row_pos, row_count)
    square = lax.psum(square_part, "rep")
    square_low = square.astype(jnp.bfloat16)
    gathered = lax.all_gather(square_low, "col", axis=1, tiled=True)
    grouped = gathered.reshape(SLAB_DEV, row_count, rep_count, block_size)
    picked = lax.dynamic_index_in_dim(grouped, rep_pos, 2, keepdims=False)
    left_second = picked.reshape(SLAB_DEV, row_count * block_size)
    cube_part, unused = cycle_product(left_second, masked, 1, row_pos, row_count)
    cube = lax.psum_scatter(cube_part, "rep", scatter_dimension=1, tiled=True)
    share_cols = tile_cols // rep_count
    square_share = lax.dynamic_slice_in_dim(square, rep_pos * share_cols, share_cols, 1)
    return 3.0 * square_share - 2.0 * cube


def solution(mesh):
    return jax.shard_map(
        local,
        mesh=mesh,
        in_specs=(P(("row", "rep"), "col"), P(), P()),
        out_specs=P("row", ("col", "rep")),
        check_vma=False,
    )
```

profile of v0, /device:TPU:1, one launch (start us, length us, event | category | flops | bytes accessed | tf_op | source)
XLA Modules:
  0.0 682.3 jit_solution(17644382543324110899)
XLA Ops:
  12.0 62.4 %all-gather.3.cloned.1.call-done = bf16[128,8192]{0,1:T(8,128)(2,1)} async-done(((bf16[128,1024]{0,1:T(8,128)(2,1)}), bf16[128,8192]{0,1:T(8,128)(2,1)}) %all-gather.3.cloned.1.call-update) | async-done | bytes 2097168 | tf_op jit(solution)/shard_map/all_gather | solution.py:62
  76.9 12.2 %all-to-all-start = ((bf16[128,16,256]{0,2,1:T(8,128)(2,1)}), bf16[128,16,256]{0,2,1:T(8,128)(2,1)S(1)}, u32[]{:S(2)}, u32[]{:S(2)}) async-start(bf16[128,16,256]{0,2,1:T(8,128)(2,1)} %bitcast.2), calls=%async_computation | async-start | bytes 2097152 | tf_op jit(solution)/shard_map/all_to_all | solution.py:65
  89.4 44.0 %all-to-all-done = bf16[128,16,256]{0,2,1:T(8,128)(2,1)S(1)} async-done(((bf16[128,16,256]{0,2,1:T(8,128)(2,1)}), bf16[128,16,256]{0,2,1:T(8,128)(2,1)S(1)}, u32[]{:S(2)}, u32[]{:S(2)}) %all-to-all-start) | async-done | bytes 1048608 | tf_op jit(solution)/shard_map/all_to_all | solution.py:65
  134.8 141.7 %while.30 = (s32[]{:T(128)}, bf16[128,1024]{1,0:T(8,128)(2,1)S(1)}, f32[256,1024]{1,0:T(8,128)S(1)}, s32[15]{0:T(128)S(1)}, s32[]{:T(128)}, /*index=5*/bf16[2048...) while((s32[]{:T(128)}, bf16[128,1024]{1,0:T(8,128)(2,1)S(1)}, ...), condition=%wide.region_2.3_spmd.clone, body=%wide.region_1.2_spmd.clone.sunk | while | flops 67633168 | bytes 3998046 | solution.py:32
  148.9 6.9 %collective-permute-done = bf16[128,1024]{1,0:T(8,128)(2,1)S(1)} collective-permute-done((bf16[128,1024]{1,0:T(8,128)(2,1)S(1)}, bf16[128,1024]{1,0:T(8,128)(2,1)S(1)}, u32[]{:S(2)}, u32[]{:S(2)}) %collective-permute-start) | collective-permute-done | bytes 262176 | tf_op jit(solution)/shard_map/while/body/eval_jaxpr/ppermute | solution.py:12
  160.2 6.0 collective-permute-done
  170.7 5.1 collective-permute-done
  213.7 4.6 collective-permute-done
  222.7 5.7 collective-permute-done
  232.9 6.8 %collective-permute-done = bf16[128,1024]{1,0:T(8,128)(2,1)S(1)} collective-permute-done((bf16[128,1024]{1,0:T(8,128)(2,1)S(1)}, bf16[128,1024]{1,0:T(8,128)(2,1)S(1)}, u32[]{:S(2)}, u32[]{:S(2)}) %collective-permute-start) | collective-permute-done | bytes 262176 | tf_op jit(solution)/shard_map/while/body/eval_jaxpr/ppermute | solution.py:12
  244.2 6.0 collective-permute-done
  254.7 5.1 collective-permute-done
  278.7 75.9 %all-reduce.2.cloned.1.call-done = f32[256,1024]{1,0:T(8,128)} async-done(((f32[256,1024]{1,0:T(8,128)}), f32[256,1024]{1,0:T(8,128)}) %all-reduce.2.cloned.1.call-update) | async-done | bytes 1048592 | tf_op jit(solution)/shard_map/psum | solution.py:67
  356.7 96.9 %all-gather.5.cloned.1.call-done = bf16[256,8192]{1,0:T(8,128)(2,1)} async-done(((bf16[256,1024]{1,0:T(8,128)(2,1)}), bf16[256,8192]{1,0:T(8,128)(2,1)}) %all-gather.5.cloned.1.call-update) | async-done | bytes 4194320 | tf_op jit(solution)/shard_map/all_gather | solution.py:69
  453.7 7.8 %reshape.14 = bf16[256,16,4,128]{3,2,1,0:T(4,128)(2,1)} reshape(bf16[256,8192]{1,0:T(8,128)(2,1)} %all-gather.5.cloned.1.call-done) | data formatting | bytes 8388608 | tf_op jit(solution)/shard_map/reshape | solution.py:70
  469.6 137.4 %while.31 = (s32[]{:T(128)}, bf16[128,1024]{1,0:T(8,128)(2,1)S(1)}, f32[256,1024]{1,0:T(8,128)S(1)}, s32[15]{0:T(128)S(1)}, s32[]{:T(128)}, /*index=5*/bf16[256,...) while((s32[]{:T(128)}, bf16[128,1024]{1,0:T(8,128)(2,1)S(1)}, ...), condition=%wide.region_5.6_spmd.clone, body=%wide.region_4.5_spmd.clone.sunk | while | flops 67633168 | bytes 3998046 | solution.py:32
  475.0 5.6 collective-permute-done.1
  485.0 4.8 collective-permute-done.1
  527.7 4.8 collective-permute-done.1
  537.0 5.9 collective-permute-done.1
  547.3 6.7 collective-permute-done.1
  558.5 5.8 collective-permute-done.1
  568.7 4.9 collective-permute-done.1
  609.2 64.8 %reduce-scatter.2.cloned.1.call-done = f32[256,256]{1,0:T(8,128)} async-done(((f32[256,1024]{1,0:T(8,128)}), f32[256,256]{1,0:T(8,128)}) %reduce-scatter.2.cloned.1.call-update) | async-done | bytes 262160 | tf_op jit(solution)/shard_map/reduce_scatter | solution.py:74
  (164 shorter events, 199.2 us)
Async XLA Ops:
  6.5 67.9 %all-gather.3.cloned.1.call-start = ((), (), s32[]{:S(2)}) async-start(), calls=%async_computation.2 | async-start | bytes 2359296 | tf_op jit(solution)/shard_map/all_gather | solution.py:62
  76.9 56.5 %all-to-all-start = ((bf16[128,16,256]{0,2,1:T(8,128)(2,1)}), bf16[128,16,256]{0,2,1:T(8,128)(2,1)S(1)}, u32[]{:S(2)}, u32[]{:S(2)}) async-start(bf16[128,16,256]{0,2,1:T(8,128)(2,1)} %bitcast.2), calls=%async_computation | async-start | bytes 2097152 | tf_op jit(solution)/shard_map/all_to_all | solution.py:65
  89.2 265.4 %all-reduce.2.cloned.1.call-start = ((), (), s32[]{:S(2)}) async-start(), calls=%async_computation.3 | async-start | bytes 2097152 | tf_op jit(solution)/shard_map/psum | solution.py:67
  134.8 9.6 %collective-permute-start = (bf16[128,1024]{1,0:T(8,128)(2,1)S(1)}, bf16[128,1024]{1,0:T(8,128)(2,1)S(1)}, u32[]{:S(2)}, u32[]{:S(2)}) collective-permute-start(bf16[128,1024]{1,0:T(8,128)(2,1)S(1)} %copy.21), channel_id=1, source_target_pairs={{0,32},{32,64},{64,96},{96,128},{128,160},{160,192},{192,224},{224... | collective-permute-start | bytes 786440 | tf_op jit(solution)/shard_map/while/body/eval_jaxpr/ppermute | solution.py:12
  144.4 11.3 %collective-permute-start = (bf16[128,1024]{1,0:T(8,128)(2,1)S(1)}, bf16[128,1024]{1,0:T(8,128)(2,1)S(1)}, u32[]{:S(2)}, u32[]{:S(2)}) collective-permute-start(bf16[128,1024]{1,0:T(8,128)(2,1)S(1)} %copy.21), channel_id=1, source_target_pairs={{0,32},{32,64},{64,96},{96,128},{128,160},{160,192},{192,224},{224... | collective-permute-start | bytes 786440 | tf_op jit(solution)/shard_map/while/body/eval_jaxpr/ppermute | solution.py:12
  155.8 10.5 %collective-permute-start = (bf16[128,1024]{1,0:T(8,128)(2,1)S(1)}, bf16[128,1024]{1,0:T(8,128)(2,1)S(1)}, u32[]{:S(2)}, u32[]{:S(2)}) collective-permute-start(bf16[128,1024]{1,0:T(8,128)(2,1)S(1)} %copy.21), channel_id=1, source_target_pairs={{0,32},{32,64},{64,96},{96,128},{128,160},{160,192},{192,224},{224... | collective-permute-start | bytes 786440 | tf_op jit(solution)/shard_map/while/body/eval_jaxpr/ppermute | solution.py:12
  166.3 9.5 %collective-permute-start = (bf16[128,1024]{1,0:T(8,128)(2,1)S(1)}, bf16[128,1024]{1,0:T(8,128)(2,1)S(1)}, u32[]{:S(2)}, u32[]{:S(2)}) collective-permute-start(bf16[128,1024]{1,0:T(8,128)(2,1)S(1)} %copy.21), channel_id=1, source_target_pairs={{0,32},{32,64},{64,96},{96,128},{128,160},{160,192},{192,224},{224... | collective-permute-start | bytes 786440 | tf_op jit(solution)/shard_map/while/body/eval_jaxpr/ppermute | solution.py:12
  175.8 8.3 %collective-permute-start = (bf16[128,1024]{1,0:T(8,128)(2,1)S(1)}, bf16[128,1024]{1,0:T(8,128)(2,1)S(1)}, u32[]{:S(2)}, u32[]{:S(2)}) collective-permute-start(bf16[128,1024]{1,0:T(8,128)(2,1)S(1)} %copy.21), channel_id=1, source_target_pairs={{0,32},{32,64},{64,96},{96,128},{128,160},{160,192},{192,224},{224... | collective-permute-start | bytes 786440 | tf_op jit(solution)/shard_map/while/body/eval_jaxpr/ppermute | solution.py:12
  184.2 8.3 %collective-permute-start = (bf16[128,1024]{1,0:T(8,128)(2,1)S(1)}, bf16[128,1024]{1,0:T(8,128)(2,1)S(1)}, u32[]{:S(2)}, u32[]{:S(2)}) collective-permute-start(bf16[128,1024]{1,0:T(8,128)(2,1)S(1)} %copy.21), channel_id=1, source_target_pairs={{0,32},{32,64},{64,96},{96,128},{128,160},{160,192},{192,224},{224... | collective-permute-start | bytes 786440 | tf_op jit(solution)/shard_map/while/body/eval_jaxpr/ppermute | solution.py:12
  192.5 8.3 %collective-permute-start = (bf16[128,1024]{1,0:T(8,128)(2,1)S(1)}, bf16[128,1024]{1,0:T(8,128)(2,1)S(1)}, u32[]{:S(2)}, u32[]{:S(2)}) collective-permute-start(bf16[128,1024]{1,0:T(8,128)(2,1)S(1)} %copy.21), channel_id=1, source_target_pairs={{0,32},{32,64},{64,96},{96,128},{128,160},{160,192},{192,224},{224... | collective-permute-start | bytes 786440 | tf_op jit(solution)/shard_map/while/body/eval_jaxpr/ppermute | solution.py:12
  209.2 9.0 %collective-permute-start = (bf16[128,1024]{1,0:T(8,128)(2,1)S(1)}, bf16[128,1024]{1,0:T(8,128)(2,1)S(1)}, u32[]{:S(2)}, u32[]{:S(2)}) collective-permute-start(bf16[128,1024]{1,0:T(8,128)(2,1)S(1)} %copy.21), channel_id=1, source_target_pairs={{0,32},{32,64},{64,96},{96,128},{128,160},{160,192},{192,224},{224... | collective-permute-start | bytes 786440 | tf_op jit(solution)/shard_map/while/body/eval_jaxpr/ppermute | solution.py:12
  218.3 10.1 %collective-permute-start = (bf16[128,1024]{1,0:T(8,128)(2,1)S(1)}, bf16[128,1024]{1,0:T(8,128)(2,1)S(1)}, u32[]{:S(2)}, u32[]{:S(2)}) collective-permute-start(bf16[128,1024]{1,0:T(8,128)(2,1)S(1)} %copy.21), channel_id=1, source_target_pairs={{0,32},{32,64},{64,96},{96,128},{128,160},{160,192},{192,224},{224... | collective-permute-start | bytes 786440 | tf_op jit(solution)/shard_map/while/body/eval_jaxpr/ppermute | solution.py:12
  228.4 11.3 %collective-permute-start = (bf16[128,1024]{1,0:T(8,128)(2,1)S(1)}, bf16[128,1024]{1,0:T(8,128)(2,1)S(1)}, u32[]{:S(2)}, u32[]{:S(2)}) collective-permute-start(bf16[128,1024]{1,0:T(8,128)(2,1)S(1)} %copy.21), channel_id=1, source_target_pairs={{0,32},{32,64},{64,96},{96,128},{128,160},{160,192},{192,224},{224... | collective-permute-start | bytes 786440 | tf_op jit(solution)/shard_map/while/body/eval_jaxpr/ppermute | solution.py:12
  239.7 10.4 %collective-permute-start = (bf16[128,1024]{1,0:T(8,128)(2,1)S(1)}, bf16[128,1024]{1,0:T(8,128)(2,1)S(1)}, u32[]{:S(2)}, u32[]{:S(2)}) collective-permute-start(bf16[128,1024]{1,0:T(8,128)(2,1)S(1)} %copy.21), channel_id=1, source_target_pairs={{0,32},{32,64},{64,96},{96,128},{128,160},{160,192},{192,224},{224... | collective-permute-start | bytes 786440 | tf_op jit(solution)/shard_map/while/body/eval_jaxpr/ppermute | solution.py:12
  250.2 9.5 %collective-permute-start = (bf16[128,1024]{1,0:T(8,128)(2,1)S(1)}, bf16[128,1024]{1,0:T(8,128)(2,1)S(1)}, u32[]{:S(2)}, u32[]{:S(2)}) collective-permute-start(bf16[128,1024]{1,0:T(8,128)(2,1)S(1)} %copy.21), channel_id=1, source_target_pairs={{0,32},{32,64},{64,96},{96,128},{128,160},{160,192},{192,224},{224... | collective-permute-start | bytes 786440 | tf_op jit(solution)/shard_map/while/body/eval_jaxpr/ppermute | solution.py:12
  278.6 175.0 %all-gather.5.cloned.1.call-start = ((), (), s32[]{:S(2)}) async-start(), calls=%async_computation.4 | async-start | bytes 4718592 | tf_op jit(solution)/shard_map/all_gather | solution.py:69
  356.7 317.3 %reduce-scatter.2.cloned.1.call-start = ((), (), s32[]{:S(2)}) async-start(), calls=%async_computation.5 | async-start | bytes 1310720 | tf_op jit(solution)/shard_map/reduce_scatter | solution.py:74
  469.6 10.9 %collective-permute-start.1 = (bf16[128,1024]{1,0:T(8,128)(2,1)S(1)}, bf16[128,1024]{1,0:T(8,128)(2,1)S(1)}, u32[]{:S(2)}, u32[]{:S(2)}) collective-permute-start(bf16[128,1024]{1,0:T(8,128)(2,1)S(1)} %copy.31), channel_id=1, source_target_pairs={{0,32},{32,64},{64,96},{96,128},{128,160},{160,192},{192,224},{224... | collective-permute-start | bytes 786440 | tf_op jit(solution)/shard_map/while/body/eval_jaxpr/ppermute | solution.py:12
  480.5 9.2 %collective-permute-start.1 = (bf16[128,1024]{1,0:T(8,128)(2,1)S(1)}, bf16[128,1024]{1,0:T(8,128)(2,1)S(1)}, u32[]{:S(2)}, u32[]{:S(2)}) collective-permute-start(bf16[128,1024]{1,0:T(8,128)(2,1)S(1)} %copy.31), channel_id=1, source_target_pairs={{0,32},{32,64},{64,96},{96,128},{128,160},{160,192},{192,224},{224... | collective-permute-start | bytes 786440 | tf_op jit(solution)/shard_map/while/body/eval_jaxpr/ppermute | solution.py:12
  523.2 9.3 %collective-permute-start.1 = (bf16[128,1024]{1,0:T(8,128)(2,1)S(1)}, bf16[128,1024]{1,0:T(8,128)(2,1)S(1)}, u32[]{:S(2)}, u32[]{:S(2)}) collective-permute-start(bf16[128,1024]{1,0:T(8,128)(2,1)S(1)} %copy.31), channel_id=1, source_target_pairs={{0,32},{32,64},{64,96},{96,128},{128,160},{160,192},{192,224},{224... | collective-permute-start | bytes 786440 | tf_op jit(solution)/shard_map/while/body/eval_jaxpr/ppermute | solution.py:12
  532.5 10.4 %collective-permute-start.1 = (bf16[128,1024]{1,0:T(8,128)(2,1)S(1)}, bf16[128,1024]{1,0:T(8,128)(2,1)S(1)}, u32[]{:S(2)}, u32[]{:S(2)}) collective-permute-start(bf16[128,1024]{1,0:T(8,128)(2,1)S(1)} %copy.31), channel_id=1, source_target_pairs={{0,32},{32,64},{64,96},{96,128},{128,160},{160,192},{192,224},{224... | collective-permute-start | bytes 786440 | tf_op jit(solution)/shard_map/while/body/eval_jaxpr/ppermute | solution.py:12
  542.9 11.1 %collective-permute-start.1 = (bf16[128,1024]{1,0:T(8,128)(2,1)S(1)}, bf16[128,1024]{1,0:T(8,128)(2,1)S(1)}, u32[]{:S(2)}, u32[]{:S(2)}) collective-permute-start(bf16[128,1024]{1,0:T(8,128)(2,1)S(1)} %copy.31), channel_id=1, source_target_pairs={{0,32},{32,64},{64,96},{96,128},{128,160},{160,192},{192,224},{224... | collective-permute-start | bytes 786440 | tf_op jit(solution)/shard_map/while/body/eval_jaxpr/ppermute | solution.py:12
  554.0 10.2 %collective-permute-start.1 = (bf16[128,1024]{1,0:T(8,128)(2,1)S(1)}, bf16[128,1024]{1,0:T(8,128)(2,1)S(1)}, u32[]{:S(2)}, u32[]{:S(2)}) collective-permute-start(bf16[128,1024]{1,0:T(8,128)(2,1)S(1)} %copy.31), channel_id=1, source_target_pairs={{0,32},{32,64},{64,96},{96,128},{128,160},{160,192},{192,224},{224... | collective-permute-start | bytes 786440 | tf_op jit(solution)/shard_map/while/body/eval_jaxpr/ppermute | solution.py:12
  564.3 9.3 %collective-permute-start.1 = (bf16[128,1024]{1,0:T(8,128)(2,1)S(1)}, bf16[128,1024]{1,0:T(8,128)(2,1)S(1)}, u32[]{:S(2)}, u32[]{:S(2)}) collective-permute-start(bf16[128,1024]{1,0:T(8,128)(2,1)S(1)} %copy.31), channel_id=1, source_target_pairs={{0,32},{32,64},{64,96},{96,128},{128,160},{160,192},{192,224},{224... | collective-permute-start | bytes 786440 | tf_op jit(solution)/shard_map/while/body/eval_jaxpr/ppermute | solution.py:12
  (12 other events, 168.8 us)
Sparse Core Ops, SparseCore 0:
  11.5 62.9 all-gather.2
  278.8 75.7 all-reduce.1
  356.8 96.7 all-gather.4
  609.3 64.6 reduce-scatter.1
where the time goes:
time: 685 us; the launch traced here: 682 us
  waiting for transfers between devices  486 us (71%)
  starting transfers between devices  73.1 us (11%)
  matrix products  41.4 us (6%)
  local copies, waits for them, and re-layouts  40 us (6%)
  loops' own time  20.5 us (3%)
  between operations  13.9 us (2%)
  other arithmetic  7.46 us (1%)
    ppermute x30, waiting for transfers between devices, from_behind(): return lax.ppermute(value, axis, pairs)  142 us
    all_gather x1, waiting for transfers between devices, local(): gathered = lax.all_gather(square_low, 'col', axis=1, tiled=True)  96.9 us
    psum x1, waiting for transfers between devices, local(): square = lax.psum(square_part, 'rep')  75.9 us
    reduce_scatter x1, waiting for transfers between devices, local(): cube = lax.psum_scatter(cube_part, 'rep', scatter_dimension=1, tiled=True)  64.8 us
    all_gather x1, waiting for transfers between devices, local(): full_rows = lax.all_gather(masked, 'col', axis=1, tiled=True)  62.4 us
    ppermute x30, starting transfers between devices, from_behind(): return lax.ppermute(value, axis, pairs)  60.7 us
    all_to_all x1, waiting for transfers between devices, local(): lax.all_to_all(slab_part, 'row', split_axis=1, concat_axis=0, tiled=True)  44 us
    dot_general x32, matrix products, partial_value(): lax.dot_general(left_rows, current, contract, preferred_element_type=jnp....  41.4 us
  transfers between devices with their start and end apart: 35, of which 35 were waited for; matrix products, arithmetic and copies ran while one was open for 8% of the time, Pallas kernels for 0%

commit v1 on v0

v1 whole, which is shorter than its diff:
```python
import jax
import jax.numpy as jnp
from jax import lax
from jax.experimental import pallas as pl
from jax.experimental.pallas import tpu as pltpu
from jax.sharding import PartitionSpec as P

BLOCK = 128
PANEL = 256
WIDE = 512
PLANES = 16
CHIPS = 16
SIDE = 4
BLOCKS = 64
MESH = pl.DeviceIdType.MESH
F32 = jnp.float32
BF16 = jnp.bfloat16


def rem(value, count):
    return lax.rem(value + count, count)


def half_piece(chip, half):
    return (chip, pl.ds(half * 128, 128))


def quarter_piece(chip, half, quarter):
    return (chip, pl.ds(half * 128 + quarter * 64, 64))


def kernel(
    density_ref, reach_ref, start_ref, out_ref,
    staged, panel, slab, square_low, extract, extract_in, part, part_in, cube_in, square,
    swap_send, swap_recv, ring_send, ring_recv, pair_send, pair_recv, plane_send, plane_recv,
):
    z = lax.axis_index("row")
    col = lax.axis_index("col")
    rep = lax.axis_index("rep")
    x, y_low = lax.div(col, 2), lax.rem(col, 2)
    y_high, core = lax.div(rep, 2), lax.rem(rep, 2)
    y = y_high * 2 + y_low
    other = 1 - core

    def chip_device(x_to, y_to):
        return (z, x_to * 2 + lax.rem(y_to, 2), lax.div(y_to, 2) * 2 + core)

    def chip_index(x_to, y_to):
        return x_to * 4 + lax.rem(y_to, 2) * 2 + lax.div(y_to, 2)

    def step(axis, offset):
        if axis == 0:
            return rem(x + offset, SIDE), y
        return x, rem(y + offset, SIDE)

    def place(first, first_offset, second_offset):
        if first == 0:
            return chip_index(rem(x + first_offset, SIDE), rem(y + second_offset, SIDE))
        return chip_index(rem(x + second_offset, SIDE), rem(y + first_offset, SIDE))

    up = (rem(z + 1, PLANES), col, rep)
    down = (rem(z - 1, PLANES), col, rep)
    sibling = (z, col, y_high * 2 + other)
    chip = chip_index(x, y)

    barrier = pltpu.get_barrier_semaphore()
    partners = [up, down]
    for axis in (0, 1):
        for offset in (1, -1):
            partners.append(chip_device(*step(axis, offset)))
    for offset in (1, 2, 3):
        partners.append((z, col, rem(rep + offset, 4)))
    for partner in partners:
        pl.semaphore_signal(barrier, inc=1, device_id=partner, device_id_type=MESH)

    own_block = z * 4 + rep
    own_reach = reach_ref[own_block]
    for block in range(8):
        column_block = col * 8 + block
        spread = lax.abs(column_block - own_block)
        spread = lax.min(spread, BLOCKS - spread)
        kept = spread <= lax.min(reach_ref[column_block], own_reach)
        scale = jnp.where(kept, 1.0, 0.0).astype(F32)
        values = density_ref[:, block * BLOCK:(block + 1) * BLOCK].astype(F32) * scale
        place_at = pl.ds((block % 4) * BLOCK, BLOCK)
        staged[block // 4, :, place_at] = values.astype(BF16)
    pl.semaphore_wait(barrier, len(partners))

    stays = y_high == core

    def swap_copy(side, sender):
        return pltpu.make_async_remote_copy(
            src_ref=staged.at[side],
            dst_ref=panel.at[z, pl.ds(sender * BLOCK, BLOCK)],
            send_sem=swap_send.at[side],
            recv_sem=swap_recv.at[sender],
            device_id=(z, col, side * 2 + y_high),
            device_id_type=MESH,
        )

    for side in (0, 1):
        is_own = jnp.logical_and(stays, y_high == side)

        @pl.when(jnp.logical_not(is_own))
        def _():
            swap_copy(side, core).start()

        @pl.when(is_own)
        def _():
            panel[z, pl.ds(side * BLOCK, BLOCK), :] = staged[side]

    for sender in (0, 1):
        is_own = jnp.logical_and(stays, core == sender)

        @pl.when(jnp.logical_not(is_own))
        def _():
            swap_copy(sender, sender).wait_recv()

    def ring_copy(way, distance, part_index):
        behind = distance - 1
        slot = rem(z - behind, PLANES) if way == 0 else rem(z + behind, PLANES)
        return pltpu.make_async_remote_copy(
            src_ref=panel.at[slot, pl.ds(part_index * 128, 128)],
            dst_ref=panel.at[slot, pl.ds(part_index * 128, 128)],
            send_sem=ring_send.at[way, behind, part_index],
            recv_sem=ring_recv.at[way, behind, part_index],
            device_id=up if way == 0 else down,
            device_id_type=MESH,
        )

    both = [(way, part_index) for part_index in (0, 1) for way in (0, 1)]
    last = [(0, 0), (1, 1)]
    for way, part_index in both:
        ring_copy(way, 1, part_index).start()

    def ring_step(distance, carry):
        for way, part_index in both:
            ring_copy(way, distance - 1, part_index).wait_recv()
            ring_copy(way, distance, part_index).start()
        return carry

    lax.fori_loop(2, 8, ring_step, 0)
    for way, part_index in last:
        ring_copy(way, 7, part_index).wait_recv()
        ring_copy(way, 8, part_index).start()
    for way, part_index in both:
        if (way, part_index) not in last:
            ring_copy(way, 7, part_index).wait_recv()
    for way, part_index in last:
        ring_copy(way, 8, part_index).wait_recv()

    first_row = start_ref[0] + z * PANEL
    first_block = lax.div(first_row, PANEL)
    inside = lax.rem(first_row, PANEL)
    mine = lax.rem(first_block, 2) == core
    held = jnp.where(mine, lax.div(first_block, 2), lax.min(lax.div(first_block + 1, 2), PLANES - 1))
    shift = jnp.where(mine, inside, inside - PANEL)
    rows = lax.broadcasted_iota(jnp.int32, (PANEL, PANEL), 0)
    columns = lax.broadcasted_iota(jnp.int32, (PANEL, PANEL), 1)
    pick = jnp.where(columns == rows + shift, 1.0, 0.0).astype(BF16)
    for side in (0, 1):
        block = panel[held, :, side * PANEL:(side + 1) * PANEL]
        extract[side] = jnp.dot(pick, block, preferred_element_type=F32).astype(BF16)

    def pair_copy(index, source, target):
        return pltpu.make_async_remote_copy(
            src_ref=source.at[other],
            dst_ref=target,
            send_sem=pair_send.at[index],
            recv_sem=pair_recv.at[index],
            device_id=sibling,
            device_id_type=MESH,
        )

    extract_copy = pair_copy(0, extract, extract_in)
    extract_copy.start()
    extract_copy.wait()
    slab[chip] = extract[core] + extract_in[...]

    def gather(phase, buffer):
        started = []
        numbers = iter(range(40))

        def send(piece_of, axis, way):
            number = next(numbers)
            mine_at, theirs_at = piece_of(0), piece_of(way)
            sent = pltpu.make_async_remote_copy(
                src_ref=buffer.at[mine_at],
                dst_ref=buffer.at[mine_at],
                send_sem=plane_send.at[phase, number],
                recv_sem=plane_recv.at[phase, number],
                device_id=chip_device(*step(axis, way)),
                device_id_type=MESH,
            )
            sent.start()
            arrives = pltpu.make_async_remote_copy(
                src_ref=buffer.at[theirs_at],
                dst_ref=buffer.at[theirs_at],
                send_sem=plane_send.at[phase, number],
                recv_sem=plane_recv.at[phase, number],
                device_id=chip_device(*step(axis, way)),
                device_id_type=MESH,
            )
            started.append(sent)
            return arrives

        ways = (1, -1)
        halves = (0, 1)
        along_first = {}
        for half in halves:
            for way in ways:
                along_first[half, way] = send(
                    lambda back, half=half: half_piece(place(half, -back, 0), half), half, way)
        along_second = {}

        def send_second(half, offset):
            for way in ways:
                along_second[half, offset, way] = send(
                    lambda back: half_piece(place(half, offset, -back), half), 1 - half, way)

        for half in halves:
            send_second(half, 0)
        far_first = {}
        for half in halves:
            for way in ways:
                along_first[half, way].wait_recv()
                quarter = 0 if way == 1 else 1
                far_first[half, way] = send(
                    lambda back: quarter_piece(place(half, -way - back, 0), half, quarter), half, way)
                send_second(half, -way)
        for half in halves:
            for way in ways:
                far_first[half, way].wait_recv()
            send_second(half, 2)
        far_second = []
        for offset in (0, -1, 1, 2):
            for half in halves:
                for way in ways:
                    along_second[half, offset, way].wait_recv()
                    quarter = 0 if way == 1 else 1
                    far_second.append(send(
                        lambda back: quarter_piece(place(half, offset, -way - back), half, quarter),
                        1 - half, way))
        for arrives in far_second:
            arrives.wait_recv()
        return started

    def product(buffer):
        part[...] = jnp.zeros_like(part)

        def add(index, carry):
            left = buffer[index]
            for side in (0, 1):
                part[side] += jnp.dot(
                    left, panel[index, :, side * PANEL:(side + 1) * PANEL], preferred_element_type=F32)
            return carry

        lax.fori_loop(0, CHIPS, add, 0)

    slab_sent = gather(0, slab)
    product(slab)
    square_copy = pair_copy(1, part, part_in)
    square_copy.start()
    square_copy.wait()
    square[...] = part[core] + part_in[...]
    square_low[chip] = square[...].astype(BF16)
    square_sent = gather(1, square_low)
    product(square_low)
    cube_copy = pair_copy(2, part, cube_in)
    cube_copy.start()
    cube_copy.wait()
    out_ref[...] = 3.0 * square[...] - 2.0 * (part[core] + cube_in[...])

    for side in (0, 1):
        @pl.when(jnp.logical_not(jnp.logical_and(stays, y_high == side)))
        def _():
            swap_copy(side, core).wait_send()

    def ring_sent(distance, carry):
        for way, part_index in both:
            ring_copy(way, distance, part_index).wait_send()
        return carry

    lax.fori_loop(1, 8, ring_sent, 0)
    for way, part_index in last:
        ring_copy(way, 8, part_index).wait_send()
    for sent in slab_sent + square_sent:
        sent.wait_send()


def local(density, reach, slab_start):
    dma = pltpu.SemaphoreType.DMA
    vmem = pl.BlockSpec(memory_space=pltpu.VMEM)
    smem = pl.BlockSpec(memory_space=pltpu.SMEM)
    return pl.pallas_call(
        kernel,
        out_shape=jax.ShapeDtypeStruct((PANEL, PANEL), F32),
        in_specs=[vmem, smem, smem],
        out_specs=vmem,
        scratch_shapes=[
            pltpu.VMEM((2, BLOCK, WIDE), BF16),
            pltpu.VMEM((PLANES, PANEL, WIDE), BF16),
            pltpu.VMEM((CHIPS, PANEL, PANEL), BF16),
            pltpu.VMEM((CHIPS, PANEL, PANEL), BF16),
            pltpu.VMEM((2, PANEL, PANEL), BF16),
            pltpu.VMEM((PANEL, PANEL), BF16),
            pltpu.VMEM((2, PANEL, PANEL), F32),
            pltpu.VMEM((PANEL, PANEL), F32),
            pltpu.VMEM((PANEL, PANEL), F32),
            pltpu.VMEM((PANEL, PANEL), F32),
            dma((2,)), dma((2,)),
            dma((2, 8, 2)), dma((2, 8, 2)),
            dma((3,)), dma((3,)),
            dma((2, 40)), dma((2, 40)),
        ],
        compiler_params=pltpu.CompilerParams(
            collective_id=0, has_side_effects=True, vmem_limit_bytes=40 * 1024 * 1024),
    )(density, reach, slab_start)


def solution(mesh):
    return jax.shard_map(
        local,
        mesh=mesh,
        in_specs=(P(("row", "rep"), "col"), P(), P()),
        out_specs=P("row", ("col", "rep")),
        check_vma=False,
    )
```

time: 685 us -> 113 us (0.16)
  waiting for transfers between devices: 486 us -> 0 us
  Pallas kernels: 0 us -> 110 us
  starting transfers between devices: 73.1 us -> 0 us
  matrix products: 41.4 us -> 0 us
  local copies, waits for them, and re-layouts: 40 us -> 1.65 us
  loops' own time: 20.5 us -> 0 us
  between operations: 13.9 us -> 0.69 us
  other arithmetic: 7.46 us -> 0 us
    all_gather x2 -> x0, waiting for transfers between devices: 159 us -> none  [the longest x1 96.9 us: local(): gathered = lax.all_gather(square_low, 'col', axis=1, tiled=True)]
    ppermute x30 -> x0, waiting for transfers between devices: 142 us -> none  [from_behind(): return lax.ppermute(value, axis, pairs)]
    pallas_call x0 -> x1, Pallas kernels: none -> 110 us  [local(): pl.pallas_call(kernel, out_shape=jax.ShapeDtypeStruct((PANEL, PANEL), F32...]
    psum x1 -> x0, waiting for transfers between devices: 75.9 us -> none  [local(): square = lax.psum(square_part, 'rep')]
    reduce_scatter x1 -> x0, waiting for transfers between devices: 64.8 us -> none  [local(): cube = lax.psum_scatter(cube_part, 'rep', scatter_dimension=1, tiled=True)]
    ppermute x30 -> x0, starting transfers between devices: 60.7 us -> none  [from_behind(): return lax.ppermute(value, axis, pairs)]
    all_to_all x1 -> x0, waiting for transfers between devices: 44 us -> none  [local(): lax.all_to_all(slab_part, 'row', split_axis=1, concat_axis=0, tiled=True)]
    dot_general x32 -> x0, matrix products: 41.4 us -> none  [partial_value(): lax.dot_general(left_rows, current, contract, preferred_element_type=jnp....]
  transfers between devices with their start and end apart: 35 -> 0, of which waited for: 35 -> 0; matrix products, arithmetic and copies ran while one was open for 8% -> 0% of each run, Pallas kernels for 0% -> 0%
where the time goes in v1:
time: 113 us; the launch traced here: 112 us
  Pallas kernels  110 us (97%)
  local copies, waits for them, and re-layouts  1.65 us (1%)
    pallas_call x1, Pallas kernels, local(): pl.pallas_call(kernel, out_shape=jax.ShapeDtypeStruct((PANEL, PANEL), F32...  110 us

profile of v1, /device:TPU:1, one launch (start us, length us, event | category | flops | bytes accessed | tf_op | source)
XLA Modules:
  0.0 112.4 jit_solution(3753169165175463006)
XLA Ops:
  0.0 0.0 copy-start.1
  0.7 0.0 copy-done.1
  0.7 0.0 copy-start
  0.7 0.9 copy-done
  1.6 110.1 %shard_map.37 = f32[256,256]{1,0:T(8,128)S(1)} custom-call(bf16[128,1024]{1,0:T(8,128)(2,1)S(1)} %copy-done, s32[64]{0:T(128)S(1)} %copy-done.1, s32[1]{0:T(128)S(6)} %copy.5.start_ref), custom_call_target="tpu_custom_call" | custom-call | tf_op jit(solution)/shard_map/pallas_call | solution.py:295
  111.7 0.7 copy.6
Async XLA Ops:
  0.0 0.7 copy-start.1
  0.7 1.0 copy-start

commit v2 on v1

v2 whole, which is shorter than its diff:
```python
import jax
import jax.numpy as jnp
from jax import lax
from jax.experimental import pallas as pl
from jax.experimental.pallas import tpu as pltpu
from jax.sharding import PartitionSpec as P

BLOCK = 128
PANEL = 256
WIDE = 512
PLANES = 16
CHIPS = 16
SIDE = 4
GROUP = 128
WAYS = (1, -1, 2)
BLOCKS = 64
MESH = pl.DeviceIdType.MESH
F32 = jnp.float32
BF16 = jnp.bfloat16


def rem(value, count):
    return lax.rem(value + count, count)


def kernel(
    density_hbm, reach_hbm, start_hbm, out_ref,
    density_ref, reach_ref, start_ref,
    staged, panel, slab, square_low, extract, extract_in, part, part_in, cube, cube_in, square,
    load_sem, swap_send, swap_recv, ring_send, ring_recv, pair_send, pair_recv, plane_send, plane_recv,
):
    z = lax.axis_index("row")
    col = lax.axis_index("col")
    rep = lax.axis_index("rep")
    x, y_low = lax.div(col, 2), lax.rem(col, 2)
    y_high, core = lax.div(rep, 2), lax.rem(rep, 2)
    y = y_high * 2 + y_low
    other = 1 - core

    def chip_device(x_to, y_to):
        return (z, x_to * 2 + lax.rem(y_to, 2), lax.div(y_to, 2) * 2 + core)

    def chip_index(x_to, y_to):
        return x_to * 4 + lax.rem(y_to, 2) * 2 + lax.div(y_to, 2)

    def step(axis, offset):
        if axis == 0:
            return rem(x + offset, SIDE), y
        return x, rem(y + offset, SIDE)

    def place(first, first_offset, second_offset):
        if first == 0:
            return chip_index(rem(x + first_offset, SIDE), rem(y + second_offset, SIDE))
        return chip_index(rem(x + second_offset, SIDE), rem(y + first_offset, SIDE))

    up = (rem(z + 1, PLANES), col, rep)
    down = (rem(z - 1, PLANES), col, rep)
    sibling = (z, col, y_high * 2 + other)
    chip = chip_index(x, y)

    barrier = pltpu.get_barrier_semaphore()
    partners = [up, down]
    for axis in (0, 1):
        for offset in (1, -1):
            partners.append(chip_device(*step(axis, offset)))
    partners.append(chip_device(*step(0, 2)))
    for offset in (1, 2, 3):
        partners.append((z, col, rem(rep + offset, 4)))
    for partner in partners:
        pl.semaphore_signal(barrier, inc=1, device_id=partner, device_id_type=MESH)

    loads = [
        pltpu.make_async_copy(reach_hbm, reach_ref, load_sem.at[0]),
        pltpu.make_async_copy(density_hbm, density_ref, load_sem.at[1]),
        pltpu.make_async_copy(start_hbm, start_ref, load_sem.at[2]),
    ]
    for load in loads:
        load.start()
    for load in loads:
        load.wait()
    own_block = z * 4 + rep
    own_reach = reach_ref[own_block]
    for block in range(8):
        column_block = col * 8 + block
        spread = lax.abs(column_block - own_block)
        spread = lax.min(spread, BLOCKS - spread)
        kept = spread <= lax.min(reach_ref[column_block], own_reach)
        scale = jnp.where(kept, 1.0, 0.0).astype(F32)
        values = density_ref[:, block * BLOCK:(block + 1) * BLOCK].astype(F32) * scale
        place_at = pl.ds((block % 4) * BLOCK, BLOCK)
        staged[block // 4, :, place_at] = values.astype(BF16)
    pl.semaphore_wait(barrier, len(partners))

    stays = y_high == core

    def swap_copy(side, sender, half):
        rows = half * 64
        return pltpu.make_async_remote_copy(
            src_ref=staged.at[side, pl.ds(rows, 64)],
            dst_ref=panel.at[z, pl.ds(sender * BLOCK + rows, 64)],
            send_sem=swap_send.at[side, half],
            recv_sem=swap_recv.at[sender, half],
            device_id=(z, col, side * 2 + y_high),
            device_id_type=MESH,
        )

    for side in (0, 1):
        is_own = jnp.logical_and(stays, y_high == side)

        @pl.when(jnp.logical_not(is_own))
        def _():
            for half in (0, 1):
                swap_copy(side, core, half).start()

        @pl.when(is_own)
        def _():
            panel[z, pl.ds(side * BLOCK, BLOCK), :] = staged[side]

    def ring_copy(way, distance, quarter):
        behind = distance - 1
        slot = rem(z - behind, PLANES) if way == 0 else rem(z + behind, PLANES)
        return pltpu.make_async_remote_copy(
            src_ref=panel.at[slot, pl.ds(quarter * 64, 64)],
            dst_ref=panel.at[slot, pl.ds(quarter * 64, 64)],
            send_sem=ring_send.at[way, behind, quarter],
            recv_sem=ring_recv.at[way, behind, quarter],
            device_id=up if way == 0 else down,
            device_id_type=MESH,
        )

    for quarter in range(4):
        sender = quarter // 2
        is_own = jnp.logical_and(stays, core == sender)

        @pl.when(jnp.logical_not(is_own))
        def _():
            swap_copy(sender, sender, quarter % 2).wait_recv()

        for way in (0, 1):
            ring_copy(way, 1, quarter).start()

    both = [(way, quarter) for quarter in range(4) for way in (0, 1)]
    last = [(0, 0), (1, 2), (0, 1), (1, 3)]

    def ring_step(distance, carry):
        for way, quarter in both:
            ring_copy(way, distance - 1, quarter).wait_recv()
            ring_copy(way, distance, quarter).start()
        return carry

    lax.fori_loop(2, 8, ring_step, 0)
    for way, quarter in last:
        ring_copy(way, 7, quarter).wait_recv()
        ring_copy(way, 8, quarter).start()
    for way, quarter in both:
        if (way, quarter) not in last:
            ring_copy(way, 7, quarter).wait_recv()
    for way, quarter in last:
        ring_copy(way, 8, quarter).wait_recv()

    first_row = start_ref[0] + z * PANEL
    first_block = lax.div(first_row, PANEL)
    inside = lax.rem(first_row, PANEL)
    mine = lax.rem(first_block, 2) == core
    held = jnp.where(mine, lax.div(first_block, 2), lax.min(lax.div(first_block + 1, 2), PLANES - 1))
    shift = jnp.where(mine, inside, inside - PANEL)
    block = panel[held]

    def pair_copy(index, source, target):
        return pltpu.make_async_remote_copy(
            src_ref=source,
            dst_ref=target,
            send_sem=pair_send.at[index],
            recv_sem=pair_recv.at[index],
            device_id=sibling,
            device_id_type=MESH,
        )

    groups = (0, 1)
    extracts = [pair_copy(g, extract.at[other, g], extract_in.at[g]) for g in groups]
    for g in groups:
        rows = lax.broadcasted_iota(jnp.int32, (GROUP, PANEL), 0) + g * GROUP
        columns = lax.broadcasted_iota(jnp.int32, (GROUP, PANEL), 1)
        pick = jnp.where(columns == rows + shift, 1.0, 0.0).astype(BF16)
        rows_out = jnp.dot(pick, block, preferred_element_type=F32).astype(BF16)
        extract[0, g] = rows_out[:, :PANEL]
        extract[1, g] = rows_out[:, PANEL:]
        extracts[g].start()

    class Gather:
        def __init__(self, phase, g, buffer):
            self.phase, self.g, self.buffer = phase, g, buffer
            self.count = 0
            self.sent = []
            self.first, self.second = {}, []

        def send(self, half, axis, way, mine, theirs):
            at = pl.ds(self.g * GROUP + half * 64, 64)
            target = chip_device(*step(axis, way))
            sems = dict(
                send_sem=plane_send.at[self.phase, self.g, self.count],
                recv_sem=plane_recv.at[self.phase, self.g, self.count],
                device_id=target, device_id_type=MESH)
            self.count += 1
            sent = pltpu.make_async_remote_copy(
                src_ref=self.buffer.at[mine, at], dst_ref=self.buffer.at[mine, at], **sems)
            sent.start()
            self.sent.append(sent)
            return pltpu.make_async_remote_copy(
                src_ref=self.buffer.at[theirs, at], dst_ref=self.buffer.at[theirs, at], **sems)

        def send_second(self, half, offset):
            for way in WAYS:
                self.second.append(self.send(
                    half, 1 - half, way, place(half, offset, 0), place(half, offset, -way)))

        def start(self):
            for way in WAYS:
                for half in (0, 1):
                    self.first[half, way] = self.send(
                        half, half, way, place(half, 0, 0), place(half, -way, 0))
            for half in (0, 1):
                self.send_second(half, 0)

        def middle(self):
            for way in WAYS:
                for half in (0, 1):
                    self.first[half, way].wait_recv()
                    self.send_second(half, -way)

        def finish(self):
            for arrives in self.second:
                arrives.wait_recv()

    def product(buffer, g, target):
        for first in range(0, CHIPS, 4):
            left = jnp.concatenate(
                [buffer[first + i, g * GROUP:(g + 1) * GROUP, :] for i in range(4)], axis=1)
            right = panel[first:first + 4].reshape(4 * PANEL, WIDE)
            for side in (0, 1):
                value = jnp.dot(
                    left, right[:, side * PANEL:(side + 1) * PANEL], preferred_element_type=F32)
                if first:
                    target[side, g] += value
                else:
                    target[side, g] = value

    slab_gathers = [Gather(0, g, slab) for g in groups]
    square_gathers = [Gather(1, g, square_low) for g in groups]
    squares = [pair_copy(2 + g, part.at[other, g], part_in.at[g]) for g in groups]
    cubes = [pair_copy(4 + g, cube.at[other, g], cube_in.at[g]) for g in groups]

    def slab_start(g):
        extracts[g].wait_recv()
        slab[chip, g * GROUP:(g + 1) * GROUP, :] = extract[core, g] + extract_in[g]
        slab_gathers[g].start()

    def square_part(g):
        slab_gathers[g].finish()
        product(slab, g, part)
        squares[g].start()

    def square_start(g):
        squares[g].wait_recv()
        square[g] = part[core, g] + part_in[g]
        square_low[chip, g * GROUP:(g + 1) * GROUP, :] = square[g].astype(BF16)
        square_gathers[g].start()

    def cube_part(g):
        square_gathers[g].finish()
        product(square_low, g, cube)
        cubes[g].start()

    def result(g):
        cubes[g].wait_recv()
        out_ref[g * GROUP:(g + 1) * GROUP, :] = 3.0 * square[g] - 2.0 * (cube[core, g] + cube_in[g])

    slab_start(0)
    slab_start(1)
    slab_gathers[0].middle()
    slab_gathers[1].middle()
    square_part(0)
    square_start(0)
    square_part(1)
    square_gathers[0].middle()
    square_start(1)
    square_gathers[1].middle()
    cube_part(0)
    cube_part(1)
    result(0)
    result(1)

    for side in (0, 1):
        @pl.when(jnp.logical_not(jnp.logical_and(stays, y_high == side)))
        def _():
            for half in (0, 1):
                swap_copy(side, core, half).wait_send()

    def ring_sent(distance, carry):
        for way, quarter in both:
            ring_copy(way, distance, quarter).wait_send()
        return carry

    lax.fori_loop(1, 8, ring_sent, 0)
    for way, quarter in last:
        ring_copy(way, 8, quarter).wait_send()
    for copy in extracts + squares + cubes:
        copy.wait_send()
    for gather in slab_gathers + square_gathers:
        for sent in gather.sent:
            sent.wait_send()


def local(density, reach, slab_start):
    dma = pltpu.SemaphoreType.DMA
    vmem = pl.BlockSpec(memory_space=pltpu.VMEM)
    hbm = pl.BlockSpec(memory_space=pltpu.HBM)
    return pl.pallas_call(
        kernel,
        out_shape=jax.ShapeDtypeStruct((PANEL, PANEL), F32),
        in_specs=[hbm, hbm, hbm],
        out_specs=vmem,
        scratch_shapes=[
            pltpu.VMEM((BLOCK, 8 * BLOCK), BF16),
            pltpu.SMEM((BLOCKS,), jnp.int32),
            pltpu.SMEM((1,), jnp.int32),
            pltpu.VMEM((2, BLOCK, WIDE), BF16),
            pltpu.VMEM((PLANES, PANEL, WIDE), BF16),
            pltpu.VMEM((CHIPS, PANEL, PANEL), BF16),
            pltpu.VMEM((CHIPS, PANEL, PANEL), BF16),
            pltpu.VMEM((2, 2, GROUP, PANEL), BF16),
            pltpu.VMEM((2, GROUP, PANEL), BF16),
            pltpu.VMEM((2, 2, GROUP, PANEL), F32),
            pltpu.VMEM((2, GROUP, PANEL), F32),
            pltpu.VMEM((2, 2, GROUP, PANEL), F32),
            pltpu.VMEM((2, GROUP, PANEL), F32),
            pltpu.VMEM((2, GROUP, PANEL), F32),
            dma((3,)),
            dma((2, 2)), dma((2, 2)),
            dma((2, 8, 4)), dma((2, 8, 4)),
            dma((6,)), dma((6,)),
            dma((2, 2, 30)), dma((2, 2, 30)),
        ],
        compiler_params=pltpu.CompilerParams(
            collective_id=0, has_side_effects=True, vmem_limit_bytes=40 * 1024 * 1024),
    )(density, reach, slab_start)


def solution(mesh):
    return jax.shard_map(
        local,
        mesh=mesh,
        in_specs=(P(("row", "rep"), "col"), P(), P()),
        out_specs=P("row", ("col", "rep")),
        check_vma=False,
    )
```

time: 113 us -> 103 us (0.912)
  Pallas kernels: 110 us -> 100 us
    pallas_call x1, Pallas kernels: 110 us -> 100 us  [local(): pl.pallas_call(kernel, out_shape=jax.ShapeDtypeStruct((PANEL, PANEL), F32...]
where the time goes in v2:
time: 103 us
  Pallas kernels  100 us (97%)
  local copies, waits for them, and re-layouts  1.65 us (2%)
    pallas_call x1, Pallas kernels, local(): pl.pallas_call(kernel, out_shape=jax.ShapeDtypeStruct((PANEL, PANEL), F32...  100 us

profile of v2, /device:TPU:1, one launch (start us, length us, event | category | flops | bytes accessed | tf_op | source)
XLA Modules:
  0.0 102.7 jit_solution(13763519045500269571)
XLA Ops:
  0.0 0.0 copy-start.1
  0.7 0.0 copy-done.1
  0.7 0.0 copy-start
  0.7 0.9 copy-done
  1.6 100.4 %shard_map.37 = f32[256,256]{1,0:T(8,128)S(1)} custom-call(bf16[128,1024]{1,0:T(8,128)(2,1)S(1)} %copy-done, s32[64]{0:T(128)S(1)} %copy-done.1, s32[1]{0:T(128)S(6)} %copy.5.start_hbm), custom_call_target="tpu_custom_call" | custom-call | tf_op jit(solution)/shard_map/pallas_call | solution.py:318
  102.0 0.7 copy.6
Async XLA Ops:
  0.0 0.7 copy-start.1
  0.7 1.0 copy-start

commit v3 on v2

--- a/solution.py
+++ b/solution.py
@@ -11,8 +11,12 @@
 PLANES = 16
 CHIPS = 16
 SIDE = 4
-GROUP = 128
+GROUPS = 2
+GROUP = PANEL // GROUPS
+HALF = GROUP // 2
+ORDER = (0, 2, 1, 3)
 WAYS = (1, -1, 2)
+OFFSETS = (0, -1, 1, -2)
 BLOCKS = 64
 MESH = pl.DeviceIdType.MESH
 F32 = jnp.float32
@@ -87,41 +91,32 @@
         kept = spread <= lax.min(reach_ref[column_block], own_reach)
         scale = jnp.where(kept, 1.0, 0.0).astype(F32)
         values = density_ref[:, block * BLOCK:(block + 1) * BLOCK].astype(F32) * scale
-        place_at = pl.ds((block % 4) * BLOCK, BLOCK)
+        place_at = pl.ds(ORDER[block % 4] * BLOCK, BLOCK)
         staged[block // 4, :, place_at] = values.astype(BF16)
     pl.semaphore_wait(barrier, len(partners))
 
-    stays = y_high == core
-
-    def swap_copy(side, sender, half):
+    def swap_copy(half):
         rows = half * 64
         return pltpu.make_async_remote_copy(
-            src_ref=staged.at[side, pl.ds(rows, 64)],
-            dst_ref=panel.at[z, pl.ds(sender * BLOCK + rows, 64)],
-            send_sem=swap_send.at[side, half],
-            recv_sem=swap_recv.at[sender, half],
-            device_id=(z, col, side * 2 + y_high),
+            src_ref=staged.at[1 - y_high, pl.ds(rows, 64)],
+            dst_ref=panel.at[z, y_high, pl.ds(rows, 64)],
+            send_sem=swap_send.at[half],
+            recv_sem=swap_recv.at[half],
+            device_id=(z, col, (1 - y_high) * 2 + core),
             device_id_type=MESH,
         )
 
-    for side in (0, 1):
-        is_own = jnp.logical_and(stays, y_high == side)
-
-        @pl.when(jnp.logical_not(is_own))
-        def _():
-            for half in (0, 1):
-                swap_copy(side, core, half).start()
-
-        @pl.when(is_own)
-        def _():
-            panel[z, pl.ds(side * BLOCK, BLOCK), :] = staged[side]
+    for half in (0, 1):
+        swap_copy(half).start()
+    panel[z, y_high] = staged[y_high]
 
     def ring_copy(way, distance, quarter):
         behind = distance - 1
         slot = rem(z - behind, PLANES) if way == 0 else rem(z + behind, PLANES)
+        where = panel.at[slot, y_high if quarter < 2 else 1 - y_high, pl.ds((quarter % 2) * 64, 64)]
         return pltpu.make_async_remote_copy(
-            src_ref=panel.at[slot, pl.ds(quarter * 64, 64)],
-            dst_ref=panel.at[slot, pl.ds(quarter * 64, 64)],
+            src_ref=where,
+            dst_ref=where,
             send_sem=ring_send.at[way, behind, quarter],
             recv_sem=ring_recv.at[way, behind, quarter],
             device_id=up if way == 0 else down,
@@ -129,13 +124,8 @@
         )
 
     for quarter in range(4):
-        sender = quarter // 2
-        is_own = jnp.logical_and(stays, core == sender)
-
-        @pl.when(jnp.logical_not(is_own))
-        def _():
-            swap_copy(sender, sender, quarter % 2).wait_recv()
-
+        if quarter >= 2:
+            swap_copy(quarter - 2).wait_recv()
         for way in (0, 1):
             ring_copy(way, 1, quarter).start()
 
@@ -159,12 +149,14 @@
         ring_copy(way, 8, quarter).wait_recv()
 
     first_row = start_ref[0] + z * PANEL
-    first_block = lax.div(first_row, PANEL)
-    inside = lax.rem(first_row, PANEL)
+    first_block = lax.div(first_row, BLOCK)
+    inside = lax.rem(first_row, BLOCK)
     mine = lax.rem(first_block, 2) == core
-    held = jnp.where(mine, lax.div(first_block, 2), lax.min(lax.div(first_block + 1, 2), PLANES - 1))
-    shift = jnp.where(mine, inside, inside - PANEL)
-    block = panel[held]
+    wanted = jnp.where(mine, lax.div(first_block, 2), lax.div(first_block + 1, 2))
+    held = lax.min(wanted, 2 * PLANES - 2)
+    past = (wanted - held) * BLOCK
+    flat = panel.reshape(2 * PLANES, BLOCK, WIDE)
+    block = flat[pl.ds(held, 2)].reshape(PANEL, WIDE)
 
     def pair_copy(index, source, target):
         return pltpu.make_async_remote_copy(
@@ -176,12 +168,16 @@
             device_id_type=MESH,
         )
 
-    groups = (0, 1)
+    groups = range(GROUPS)
     extracts = [pair_copy(g, extract.at[other, g], extract_in.at[g]) for g in groups]
     for g in groups:
         rows = lax.broadcasted_iota(jnp.int32, (GROUP, PANEL), 0) + g * GROUP
         columns = lax.broadcasted_iota(jnp.int32, (GROUP, PANEL), 1)
-        pick = jnp.where(columns == rows + shift, 1.0, 0.0).astype(BF16)
+        seen = rows + inside
+        middle = jnp.logical_and(seen >= BLOCK, seen < 2 * BLOCK)
+        wants = jnp.where(jnp.logical_and(mine, seen < BLOCK), seen, seen - BLOCK) + past
+        taken = jnp.logical_and(columns == wants, middle != mine)
+        pick = jnp.where(taken, 1.0, 0.0).astype(BF16)
         rows_out = jnp.dot(pick, block, preferred_element_type=F32).astype(BF16)
         extract[0, g] = rows_out[:, :PANEL]
         extract[1, g] = rows_out[:, PANEL:]
@@ -192,10 +188,10 @@
             self.phase, self.g, self.buffer = phase, g, buffer
             self.count = 0
             self.sent = []
-            self.first, self.second = {}, []
+            self.first, self.second = {}, {}
 
         def send(self, half, axis, way, mine, theirs):
-            at = pl.ds(self.g * GROUP + half * 64, 64)
+            at = pl.ds(self.g * GROUP + half * HALF, HALF)
             target = chip_device(*step(axis, way))
             sems = dict(
                 send_sem=plane_send.at[self.phase, self.g, self.count],
@@ -210,9 +206,9 @@
                 src_ref=self.buffer.at[theirs, at], dst_ref=self.buffer.at[theirs, at], **sems)
 
         def send_second(self, half, offset):
-            for way in WAYS:
-                self.second.append(self.send(
-                    half, 1 - half, way, place(half, offset, 0), place(half, offset, -way)))
+            for way in (1, -1):
+                self.second[half, offset, way] = self.send(
+                    half, 1 - half, way, place(half, offset, 0), place(half, offset, -way))
 
         def start(self):
             for way in WAYS:
@@ -228,8 +224,16 @@
                     self.first[half, way].wait_recv()
                     self.send_second(half, -way)
 
+        def forward(self):
+            for offset in OFFSETS:
+                way = 1 if offset in (0, -2) else -1
+                for half in (0, 1):
+                    self.second.pop((half, offset, way)).wait_recv()
+                    self.second[half, offset] = self.send(
+                        half, 1 - half, way, place(half, offset, -way), place(half, offset, -2 * way))
+
         def finish(self):
-            for arrives in self.second:
+            for arrives in self.second.values():
                 arrives.wait_recv()
 
     def product(buffer, g, target):
@@ -247,8 +251,8 @@
 
     slab_gathers = [Gather(0, g, slab) for g in groups]
     square_gathers = [Gather(1, g, square_low) for g in groups]
-    squares = [pair_copy(2 + g, part.at[other, g], part_in.at[g]) for g in groups]
-    cubes = [pair_copy(4 + g, cube.at[other, g], cube_in.at[g]) for g in groups]
+    squares = [pair_copy(GROUPS + g, part.at[other, g], part_in.at[g]) for g in groups]
+    cubes = [pair_copy(2 * GROUPS + g, cube.at[other, g], cube_in.at[g]) for g in groups]
 
     def slab_start(g):
         extracts[g].wait_recv()
@@ -268,33 +272,40 @@
 
     def cube_part(g):
         square_gathers[g].finish()
-        product(square_low, g, cube)
+        squares[g].wait_send()
+        product(square_low, g, part)
+        for colour in (0, 1):
+            own = jnp.where(core == colour, 3.0, 0.0)
+            value = own * square[g] - 2.0 * part[colour, g]
+            for side in (0, 1):
+                cube[side, g, :, colour * BLOCK:(colour + 1) * BLOCK] = value[:, side * BLOCK:(side + 1) * BLOCK]
         cubes[g].start()
 
     def result(g):
         cubes[g].wait_recv()
-        out_ref[g * GROUP:(g + 1) * GROUP, :] = 3.0 * square[g] - 2.0 * (cube[core, g] + cube_in[g])
+        out_ref[g * GROUP:(g + 1) * GROUP, :] = cube[core, g] + cube_in[g]
 
     slab_start(0)
     slab_start(1)
     slab_gathers[0].middle()
     slab_gathers[1].middle()
+    slab_gathers[0].forward()
+    slab_gathers[1].forward()
     square_part(0)
     square_start(0)
     square_part(1)
+    square_start(1)
     square_gathers[0].middle()
-    square_start(1)
     square_gathers[1].middle()
+    square_gathers[0].forward()
+    square_gathers[1].forward()
     cube_part(0)
     cube_part(1)
     result(0)
     result(1)
 
-    for side in (0, 1):
-        @pl.when(jnp.logical_not(jnp.logical_and(stays, y_high == side)))
-        def _():
-            for half in (0, 1):
-                swap_copy(side, core, half).wait_send()
+    for half in (0, 1):
+        swap_copy(half).wait_send()
 
     def ring_sent(distance, carry):
         for way, quarter in both:
@@ -304,7 +315,7 @@
     lax.fori_loop(1, 8, ring_sent, 0)
     for way, quarter in last:
         ring_copy(way, 8, quarter).wait_send()
-    for copy in extracts + squares + cubes:
+    for copy in extracts + cubes:
         copy.wait_send()
     for gather in slab_gathers + square_gathers:
         for sent in gather.sent:
@@ -325,21 +336,21 @@
             pltpu.SMEM((BLOCKS,), jnp.int32),
             pltpu.SMEM((1,), jnp.int32),
             pltpu.VMEM((2, BLOCK, WIDE), BF16),
-            pltpu.VMEM((PLANES, PANEL, WIDE), BF16),
+            pltpu.VMEM((PLANES, 2, BLOCK, WIDE), BF16),
             pltpu.VMEM((CHIPS, PANEL, PANEL), BF16),
             pltpu.VMEM((CHIPS, PANEL, PANEL), BF16),
-            pltpu.VMEM((2, 2, GROUP, PANEL), BF16),
-            pltpu.VMEM((2, GROUP, PANEL), BF16),
-            pltpu.VMEM((2, 2, GROUP, PANEL), F32),
-            pltpu.VMEM((2, GROUP, PANEL), F32),
-            pltpu.VMEM((2, 2, GROUP, PANEL), F32),
-            pltpu.VMEM((2, GROUP, PANEL), F32),
-            pltpu.VMEM((2, GROUP, PANEL), F32),
+            pltpu.VMEM((2, GROUPS, GROUP, PANEL), BF16),
+            pltpu.VMEM((GROUPS, GROUP, PANEL), BF16),
+            pltpu.VMEM((2, GROUPS, GROUP, PANEL), F32),
+            pltpu.VMEM((GROUPS, GROUP, PANEL), F32),
+            pltpu.VMEM((2, GROUPS, GROUP, PANEL), F32),
+            pltpu.VMEM((GROUPS, GROUP, PANEL), F32),
+            pltpu.VMEM((GROUPS, GROUP, PANEL), F32),
             dma((3,)),
-            dma((2, 2)), dma((2, 2)),
+            dma((2,)), dma((2,)),
             dma((2, 8, 4)), dma((2, 8, 4)),
-            dma((6,)), dma((6,)),
-            dma((2, 2, 30)), dma((2, 2, 30)),
+            dma((3 * GROUPS,)), dma((3 * GROUPS,)),
+            dma((2, GROUPS, 30)), dma((2, GROUPS, 30)),
         ],
         compiler_params=pltpu.CompilerParams(
             collective_id=0, has_side_effects=True, vmem_limit_bytes=40 * 1024 * 1024),

time: 103 us -> 98 us (0.951)
  Pallas kernels: 100 us -> 95.5 us
    pallas_call x1, Pallas kernels: 100 us -> 95.5 us  [local(): pl.pallas_call(kernel, out_shape=jax.ShapeDtypeStruct((PANEL, PANEL), F32...]
where the time goes in v3:
time: 98 us; the launch traced here: 97.9 us
  Pallas kernels  95.5 us (97%)
  local copies, waits for them, and re-layouts  1.65 us (2%)
    pallas_call x1, Pallas kernels, local(): pl.pallas_call(kernel, out_shape=jax.ShapeDtypeStruct((PANEL, PANEL), F32...  95.5 us

profile of v3, /device:TPU:1, one launch (start us, length us, event | category | flops | bytes accessed | tf_op | source)
XLA Modules:
  0.0 97.9 jit_solution(17834856273337373760)
XLA Ops:
  0.0 0.0 copy-start.1
  0.7 0.0 copy-done.1
  0.7 0.0 copy-start
  0.7 0.9 copy-done
  1.6 95.5 %shard_map.37 = f32[256,256]{1,0:T(8,128)S(1)} custom-call(bf16[128,1024]{1,0:T(8,128)(2,1)S(1)} %copy-done, s32[64]{0:T(128)S(1)} %copy-done.1, s32[1]{0:T(128)S(6)} %copy.5.start_hbm), custom_call_target="tpu_custom_call" | custom-call | tf_op jit(solution)/shard_map/pallas_call | solution.py:329
  97.2 0.7 copy.6
Async XLA Ops:
  0.0 0.7 copy-start.1
  0.7 1.0 copy-start

commit v4 on v3

--- a/solution.py
+++ b/solution.py
@@ -16,6 +16,7 @@
 HALF = GROUP // 2
 ORDER = (0, 2, 1, 3)
 WAYS = (1, -1, 2)
+FIRST = (1, -1, 2)
 OFFSETS = (0, -1, 1, -2)
 BLOCKS = 64
 MESH = pl.DeviceIdType.MESH
@@ -117,7 +118,7 @@
         return pltpu.make_async_remote_copy(
             src_ref=where,
             dst_ref=where,
-            send_sem=ring_send.at[way, behind, quarter],
+            send_sem=ring_send,
             recv_sem=ring_recv.at[way, behind, quarter],
             device_id=up if way == 0 else down,
             device_id_type=MESH,
@@ -187,31 +188,35 @@
         def __init__(self, phase, g, buffer):
             self.phase, self.g, self.buffer = phase, g, buffer
             self.count = 0
-            self.sent = []
             self.first, self.second = {}, {}
 
-        def send(self, half, axis, way, mine, theirs):
+        def send(self, half, axis, way, mine, theirs, number=None):
             at = pl.ds(self.g * GROUP + half * HALF, HALF)
-            target = chip_device(*step(axis, way))
+            if number is None:
+                number = self.count
+                self.count += 1
             sems = dict(
-                send_sem=plane_send.at[self.phase, self.g, self.count],
-                recv_sem=plane_recv.at[self.phase, self.g, self.count],
-                device_id=target, device_id_type=MESH)
-            self.count += 1
-            sent = pltpu.make_async_remote_copy(
-                src_ref=self.buffer.at[mine, at], dst_ref=self.buffer.at[mine, at], **sems)
-            sent.start()
-            self.sent.append(sent)
-            return pltpu.make_async_remote_copy(
-                src_ref=self.buffer.at[theirs, at], dst_ref=self.buffer.at[theirs, at], **sems)
+                send_sem=plane_send.at[self.phase],
+                recv_sem=plane_recv.at[self.phase, self.g, number],
+                device_id=chip_device(*step(axis, way)), device_id_type=MESH)
+            pltpu.make_async_remote_copy(
+                src_ref=self.buffer.at[mine, at], dst_ref=self.buffer.at[mine, at], **sems).start()
+
+            def arrives():
+                pltpu.make_async_remote_copy(
+                    src_ref=self.buffer.at[theirs, at], dst_ref=self.buffer.at[theirs, at], **sems).wait_recv()
+
+            return arrives
 
         def send_second(self, half, offset):
+            onward = 1 if offset in (0, -2) else -1
             for way in (1, -1):
                 self.second[half, offset, way] = self.send(
-                    half, 1 - half, way, place(half, offset, 0), place(half, offset, -way))
+                    half, 1 - half, way, place(half, offset, 0), place(half, offset, -way),
+                    None if way == onward else 14)
 
         def start(self):
-            for way in WAYS:
+            for way in FIRST:
                 for half in (0, 1):
                     self.first[half, way] = self.send(
                         half, half, way, place(half, 0, 0), place(half, -way, 0))
@@ -221,33 +226,53 @@
         def middle(self):
             for way in WAYS:
                 for half in (0, 1):
-                    self.first[half, way].wait_recv()
+                    self.first[half, way]()
                     self.send_second(half, -way)
 
         def forward(self):
             for offset in OFFSETS:
                 way = 1 if offset in (0, -2) else -1
                 for half in (0, 1):
-                    self.second.pop((half, offset, way)).wait_recv()
-                    self.second[half, offset] = self.send(
-                        half, 1 - half, way, place(half, offset, -way), place(half, offset, -2 * way))
+                    self.second[half, offset, way]()
+                    self.send(half, 1 - half, way, place(half, offset, -way), place(half, offset, -2 * way), 15)
+
+        def all_of(self, number):
+            pltpu.make_async_remote_copy(
+                src_ref=self.buffer.at[pl.ds(0, 2), pl.ds(0, PANEL)],
+                dst_ref=self.buffer.at[pl.ds(0, 2), pl.ds(0, PANEL)],
+                send_sem=plane_send.at[self.phase],
+                recv_sem=plane_recv.at[self.phase, self.g, number],
+                device_id=sibling, device_id_type=MESH).wait_recv()
+
+        def near(self):
+            self.all_of(14)
 
         def finish(self):
-            for arrives in self.second.values():
-                arrives.wait_recv()
-
-    def product(buffer, g, target):
-        for first in range(0, CHIPS, 4):
-            left = jnp.concatenate(
-                [buffer[first + i, g * GROUP:(g + 1) * GROUP, :] for i in range(4)], axis=1)
-            right = panel[first:first + 4].reshape(4 * PANEL, WIDE)
-            for side in (0, 1):
-                value = jnp.dot(
-                    left, right[:, side * PANEL:(side + 1) * PANEL], preferred_element_type=F32)
-                if first:
-                    target[side, g] += value
-                else:
-                    target[side, g] = value
+            self.all_of(15)
+
+    NEAR = [(dx, dy) for dx in (0, 1, -1) for dy in (0, 1, -1)]
+    FAR = [(2, dy) for dy in (0, 1, -1, 2)] + [(dx, 2) for dx in (0, 1, -1)]
+
+    def product(buffer, g, target, offsets, first):
+        rows = pl.ds(g * GROUP, GROUP)
+        value = None
+        indices = [place(0, dx, dy) for dx, dy in offsets]
+        left = jnp.concatenate([buffer[index, rows, :] for index in indices], axis=1)
+        right = jnp.concatenate([panel[index].reshape(PANEL, WIDE) for index in indices], axis=0)
+        value = jnp.dot(left, right, preferred_element_type=F32)
+        for side in (0, 1):
+            half = value[:, side * PANEL:(side + 1) * PANEL]
+            target[side, g] = half if first else target[side, g] + half
+
+    def all_sent(array, semaphore):
+        pltpu.make_async_remote_copy(
+            src_ref=array.at[pl.ds(0, PLANES - 1)],
+            dst_ref=array.at[pl.ds(0, PLANES - 1)],
+            send_sem=semaphore,
+            recv_sem=semaphore,
+            device_id=sibling,
+            device_id_type=MESH,
+        ).wait_send()
 
     slab_gathers = [Gather(0, g, slab) for g in groups]
     square_gathers = [Gather(1, g, square_low) for g in groups]
@@ -259,9 +284,13 @@
         slab[chip, g * GROUP:(g + 1) * GROUP, :] = extract[core, g] + extract_in[g]
         slab_gathers[g].start()
 
+    def square_near(g):
+        slab_gathers[g].near()
+        product(slab, g, part, NEAR, True)
+
     def square_part(g):
         slab_gathers[g].finish()
-        product(slab, g, part)
+        product(slab, g, part, FAR, False)
         squares[g].start()
 
     def square_start(g):
@@ -270,10 +299,14 @@
         square_low[chip, g * GROUP:(g + 1) * GROUP, :] = square[g].astype(BF16)
         square_gathers[g].start()
 
+    def cube_near(g):
+        squares[g].wait_send()
+        square_gathers[g].near()
+        product(square_low, g, part, NEAR, True)
+
     def cube_part(g):
         square_gathers[g].finish()
-        squares[g].wait_send()
-        product(square_low, g, part)
+        product(square_low, g, part, FAR, False)
         for colour in (0, 1):
             own = jnp.where(core == colour, 3.0, 0.0)
             value = own * square[g] - 2.0 * part[colour, g]
@@ -287,39 +320,34 @@
 
     slab_start(0)
     slab_start(1)
+    all_sent(panel, ring_send)
+    for copy in [swap_copy(0), swap_copy(1)] + extracts:
+        copy.wait_send()
     slab_gathers[0].middle()
     slab_gathers[1].middle()
     slab_gathers[0].forward()
     slab_gathers[1].forward()
+    square_near(0)
+    square_near(1)
     square_part(0)
     square_start(0)
     square_part(1)
     square_start(1)
+    all_sent(slab, plane_send.at[0])
     square_gathers[0].middle()
     square_gathers[1].middle()
     square_gathers[0].forward()
     square_gathers[1].forward()
+    cube_near(0)
+    cube_near(1)
     cube_part(0)
     cube_part(1)
+    all_sent(square_low, plane_send.at[1])
     result(0)
     result(1)
 
-    for half in (0, 1):
-        swap_copy(half).wait_send()
-
-    def ring_sent(distance, carry):
-        for way, quarter in both:
-            ring_copy(way, distance, quarter).wait_send()
-        return carry
-
-    lax.fori_loop(1, 8, ring_sent, 0)
-    for way, quarter in last:
-        ring_copy(way, 8, quarter).wait_send()
-    for copy in extracts + cubes:
+    for copy in cubes:
         copy.wait_send()
-    for gather in slab_gathers + square_gathers:
-        for sent in gather.sent:
-            sent.wait_send()
 
 
 def local(density, reach, slab_start):
@@ -348,9 +376,9 @@
             pltpu.VMEM((GROUPS, GROUP, PANEL), F32),
             dma((3,)),
             dma((2,)), dma((2,)),
-            dma((2, 8, 4)), dma((2, 8, 4)),
+            dma, dma((2, 8, 4)),
             dma((3 * GROUPS,)), dma((3 * GROUPS,)),
-            dma((2, GROUPS, 30)), dma((2, GROUPS, 30)),
+            dma((2,)), dma((2, GROUPS, 16)),
         ],
         compiler_params=pltpu.CompilerParams(
             collective_id=0, has_side_effects=True, vmem_limit_bytes=40 * 1024 * 1024),

time: 98 us -> 95 us (0.969)
  Pallas kernels: 95.5 us -> 92.5 us
    pallas_call x1, Pallas kernels: 95.5 us -> 92.5 us  [local(): pl.pallas_call(kernel, out_shape=jax.ShapeDtypeStruct((PANEL, PANEL), F32...]
where the time goes in v4:
time: 95 us; the launch traced here: 94.8 us
  Pallas kernels  92.5 us (97%)
  local copies, waits for them, and re-layouts  1.65 us (2%)
    pallas_call x1, Pallas kernels, local(): pl.pallas_call(kernel, out_shape=jax.ShapeDtypeStruct((PANEL, PANEL), F32...  92.5 us

profile of v4, /device:TPU:1, one launch (start us, length us, event | category | flops | bytes accessed | tf_op | source)
XLA Modules:
  0.0 94.8 jit_solution(14532489851936565591)
XLA Ops:
  0.0 0.0 copy-start.1
  0.7 0.0 copy-done.1
  0.7 0.0 copy-start
  0.7 0.9 copy-done
  1.6 92.5 %shard_map.37 = f32[256,256]{1,0:T(8,128)S(1)} custom-call(bf16[128,1024]{1,0:T(8,128)(2,1)S(1)} %copy-done, s32[64]{0:T(128)S(1)} %copy-done.1, s32[1]{0:T(128)S(6)} %copy.5.start_hbm), custom_call_target="tpu_custom_call" | custom-call | tf_op jit(solution)/shard_map/pallas_call | solution.py:357
  94.1 0.7 copy.6
Async XLA Ops:
  0.0 0.7 copy-start.1
  0.7 1.0 %copy-start = (bf16[128,1024]{1,0:T(8,128)(2,1)S(1)}, bf16[128,1024]{1,0:T(8,128)(2,1)}, u32[]{:S(2)}) copy-start(bf16[128,1024]{1,0:T(8,128)(2,1)} %density_hbm.1) | copy-start | bytes 786436

commit v5 on v4

--- a/solution.py
+++ b/solution.py
@@ -124,30 +124,41 @@
             device_id_type=MESH,
         )
 
-    for quarter in range(4):
-        if quarter >= 2:
-            swap_copy(quarter - 2).wait_recv()
-        for way in (0, 1):
-            ring_copy(way, 1, quarter).start()
-
-    both = [(way, quarter) for quarter in range(4) for way in (0, 1)]
-    last = [(0, 0), (1, 2), (0, 1), (1, 3)]
-
-    def ring_step(distance, carry):
-        for way, quarter in both:
+    own = [(way, quarter) for quarter in (0, 1) for way in (0, 1)]
+    swapped = [(way, quarter) for quarter in (2, 3) for way in (0, 1)]
+
+    def hand_on(distance, pieces):
+        for way, quarter in pieces:
             ring_copy(way, distance - 1, quarter).wait_recv()
             ring_copy(way, distance, quarter).start()
+
+    def arrived(distance, pieces):
+        for way, quarter in pieces:
+            ring_copy(way, distance, quarter).wait_recv()
+
+    for way, quarter in own:
+        ring_copy(way, 1, quarter).start()
+    hand_on(2, own)
+    for way, quarter in swapped:
+        if way == 0:
+            swap_copy(quarter - 2).wait_recv()
+        ring_copy(way, 1, quarter).start()
+
+    def ring_step(distance, carry):
+        hand_on(distance + 1, own)
+        hand_on(distance, swapped)
         return carry
 
-    lax.fori_loop(2, 8, ring_step, 0)
-    for way, quarter in last:
-        ring_copy(way, 7, quarter).wait_recv()
-        ring_copy(way, 8, quarter).start()
-    for way, quarter in both:
-        if (way, quarter) not in last:
-            ring_copy(way, 7, quarter).wait_recv()
-    for way, quarter in last:
-        ring_copy(way, 8, quarter).wait_recv()
+    lax.fori_loop(2, 7, ring_step, 0)
+    own_up, own_down = [(0, 0), (0, 1)], [(1, 0), (1, 1)]
+    swapped_up, swapped_down = [(0, 2), (0, 3)], [(1, 2), (1, 3)]
+    hand_on(8, own_up)
+    hand_on(7, swapped)
+    hand_on(8, swapped_down)
+    arrived(7, own_down)
+    arrived(7, swapped_up)
+    arrived(8, own_up)
+    arrived(8, swapped_down)
 
     first_row = start_ref[0] + z * PANEL
     first_block = lax.div(first_row, BLOCK)

time: 95 us -> 94.6 us (level)
  no operation moved by 1% of the time
where the time goes in v5:
time: 94.6 us; the launch traced here: 94.5 us
  Pallas kernels  92.1 us (97%)
  local copies, waits for them, and re-layouts  1.65 us (2%)
    pallas_call x1, Pallas kernels, local(): pl.pallas_call(kernel, out_shape=jax.ShapeDtypeStruct((PANEL, PANEL), F32...  92.1 us

profile of v5, /device:TPU:1, one launch (start us, length us, event | category | flops | bytes accessed | tf_op | source)
XLA Modules:
  0.0 94.5 jit_solution(926498233244947142)
XLA Ops:
  0.0 0.0 copy-start.1
  0.7 0.0 copy-done.1
  0.7 0.0 copy-start
  0.7 0.9 copy-done
  1.6 92.1 %shard_map.37 = f32[256,256]{1,0:T(8,128)S(1)} custom-call(bf16[128,1024]{1,0:T(8,128)(2,1)S(1)} %copy-done, s32[64]{0:T(128)S(1)} %copy-done.1, s32[1]{0:T(128)S(6)} %copy.5.start_hbm), custom_call_target="tpu_custom_call" | custom-call | tf_op jit(solution)/shard_map/pallas_call | solution.py:368
  93.8 0.7 copy.6
Async XLA Ops:
  0.0 0.7 copy-start.1
  0.7 1.0 %copy-start = (bf16[128,1024]{1,0:T(8,128)(2,1)S(1)}, bf16[128,1024]{1,0:T(8,128)(2,1)}, u32[]{:S(2)}) copy-start(bf16[128,1024]{1,0:T(8,128)(2,1)} %density_hbm.1) | copy-start | bytes 786436

commit v6 on v5

--- a/solution.py
+++ b/solution.py
@@ -114,7 +114,7 @@
     def ring_copy(way, distance, quarter):
         behind = distance - 1
         slot = rem(z - behind, PLANES) if way == 0 else rem(z + behind, PLANES)
-        where = panel.at[slot, y_high if quarter < 2 else 1 - y_high, pl.ds((quarter % 2) * 64, 64)]
+        where = panel.at[slot, y_high if quarter < 4 else 1 - y_high, pl.ds((quarter % 4) * 32, 32)]
         return pltpu.make_async_remote_copy(
             src_ref=where,
             dst_ref=where,
@@ -124,8 +124,8 @@
             device_id_type=MESH,
         )
 
-    own = [(way, quarter) for quarter in (0, 1) for way in (0, 1)]
-    swapped = [(way, quarter) for quarter in (2, 3) for way in (0, 1)]
+    own = [(way, quarter) for quarter in range(4) for way in (0, 1)]
+    swapped = [(way, quarter) for quarter in range(4, 8) for way in (0, 1)]
 
     def hand_on(distance, pieces):
         for way, quarter in pieces:
@@ -140,8 +140,8 @@
         ring_copy(way, 1, quarter).start()
     hand_on(2, own)
     for way, quarter in swapped:
-        if way == 0:
-            swap_copy(quarter - 2).wait_recv()
+        if way == 0 and (quarter - 4) % 2 == 0:
+            swap_copy((quarter - 4) // 2).wait_recv()
         ring_copy(way, 1, quarter).start()
 
     def ring_step(distance, carry):
@@ -150,8 +150,8 @@
         return carry
 
     lax.fori_loop(2, 7, ring_step, 0)
-    own_up, own_down = [(0, 0), (0, 1)], [(1, 0), (1, 1)]
-    swapped_up, swapped_down = [(0, 2), (0, 3)], [(1, 2), (1, 3)]
+    own_up, own_down = own[::2], own[1::2]
+    swapped_up, swapped_down = swapped[::2], swapped[1::2]
     hand_on(8, own_up)
     hand_on(7, swapped)
     hand_on(8, swapped_down)
@@ -220,7 +220,7 @@
             return arrives
 
         def send_second(self, half, offset):
-            onward = 1 if offset in (0, -2) else -1
+            onward = 1 if offset in (0, -1) else -1
             for way in (1, -1):
                 self.second[half, offset, way] = self.send(
                     half, 1 - half, way, place(half, offset, 0), place(half, offset, -way),
@@ -242,7 +242,7 @@
 
         def forward(self):
             for offset in OFFSETS:
-                way = 1 if offset in (0, -2) else -1
+                way = 1 if offset in (0, -1) else -1
                 for half in (0, 1):
                     self.second[half, offset, way]()
                     self.send(half, 1 - half, way, place(half, offset, -way), place(half, offset, -2 * way), 15)
@@ -352,9 +352,9 @@
     cube_near(0)
     cube_near(1)
     cube_part(0)
+    result(0)
     cube_part(1)
     all_sent(square_low, plane_send.at[1])
-    result(0)
     result(1)
 
     for copy in cubes:
@@ -387,7 +387,7 @@
             pltpu.VMEM((GROUPS, GROUP, PANEL), F32),
             dma((3,)),
             dma((2,)), dma((2,)),
-            dma, dma((2, 8, 4)),
+            dma, dma((2, 8, 8)),
             dma((3 * GROUPS,)), dma((3 * GROUPS,)),
             dma((2,)), dma((2, GROUPS, 16)),
         ],

time: 94.6 us -> 93.9 us (level)
  no operation moved by 1% of the time
where the time goes in v6:
time: 93.9 us; the launch traced here: 93.8 us
  Pallas kernels  91.4 us (97%)
  local copies, waits for them, and re-layouts  1.65 us (2%)
    pallas_call x1, Pallas kernels, local(): pl.pallas_call(kernel, out_shape=jax.ShapeDtypeStruct((PANEL, PANEL), F32...  91.4 us

profile of v6, /device:TPU:1, one launch (start us, length us, event | category | flops | bytes accessed | tf_op | source)
XLA Modules:
  0.0 93.8 jit_solution(55134037073642134)
XLA Ops:
  0.0 0.0 copy-start.1
  0.7 0.0 copy-done.1
  0.7 0.0 copy-start
  0.7 0.9 %copy-done = bf16[128,1024]{1,0:T(8,128)(2,1)S(1)} copy-done((bf16[128,1024]{1,0:T(8,128)(2,1)S(1)}, bf16[128,1024]{1,0:T(8,128)(2,1)}, u32[]{:S(2)}) %copy-start) | copy-done | bytes 262168
  1.6 91.4 %shard_map.37 = f32[256,256]{1,0:T(8,128)S(1)} custom-call(bf16[128,1024]{1,0:T(8,128)(2,1)S(1)} %copy-done, s32[64]{0:T(128)S(1)} %copy-done.1, s32[1]{0:T(128)S(6)} %copy.5.start_hbm), custom_call_target="tpu_custom_call" | custom-call | tf_op jit(solution)/shard_map/pallas_call | solution.py:368
  93.1 0.7 copy.6
Async XLA Ops:
  0.0 0.7 copy-start.1
  0.7 1.0 %copy-start = (bf16[128,1024]{1,0:T(8,128)(2,1)S(1)}, bf16[128,1024]{1,0:T(8,128)(2,1)}, u32[]{:S(2)}) copy-start(bf16[128,1024]{1,0:T(8,128)(2,1)} %density_hbm.1) | copy-start | bytes 786436

commit v7 on v6

--- a/solution.py
+++ b/solution.py
@@ -29,8 +29,8 @@
 
 
 def kernel(
-    density_hbm, reach_hbm, start_hbm, out_ref,
-    density_ref, reach_ref, start_ref,
+    density_ref, reach_hbm, start_hbm, out_ref,
+    reach_ref, start_ref,
     staged, panel, slab, square_low, extract, extract_in, part, part_in, cube, cube_in, square,
     load_sem, swap_send, swap_recv, ring_send, ring_recv, pair_send, pair_recv, plane_send, plane_recv,
 ):
@@ -76,7 +76,6 @@
 
     loads = [
         pltpu.make_async_copy(reach_hbm, reach_ref, load_sem.at[0]),
-        pltpu.make_async_copy(density_hbm, density_ref, load_sem.at[1]),
         pltpu.make_async_copy(start_hbm, start_ref, load_sem.at[2]),
     ]
     for load in loads:
@@ -368,10 +367,9 @@
     return pl.pallas_call(
         kernel,
         out_shape=jax.ShapeDtypeStruct((PANEL, PANEL), F32),
-        in_specs=[hbm, hbm, hbm],
+        in_specs=[vmem, hbm, hbm],
         out_specs=vmem,
         scratch_shapes=[
-            pltpu.VMEM((BLOCK, 8 * BLOCK), BF16),
             pltpu.SMEM((BLOCKS,), jnp.int32),
             pltpu.SMEM((1,), jnp.int32),
             pltpu.VMEM((2, BLOCK, WIDE), BF16),

time: 93.9 us -> 93.9 us (level)
  no operation moved by 1% of the time
where the time goes in v7:
time: 93.9 us; the launch traced here: 93.8 us
  Pallas kernels  91.4 us (97%)
  local copies, waits for them, and re-layouts  1.65 us (2%)
    pallas_call x1, Pallas kernels, local(): pl.pallas_call(kernel, out_shape=jax.ShapeDtypeStruct((PANEL, PANEL), F32...  91.4 us

profile of v7, /device:TPU:1, one launch (start us, length us, event | category | flops | bytes accessed | tf_op | source)
XLA Modules:
  0.0 93.8 jit_solution(16693524043347796236)
XLA Ops:
  0.0 0.0 copy-start.1
  0.7 0.0 copy-done.1
  0.7 0.0 copy-start
  0.7 0.9 %copy-done = bf16[128,1024]{1,0:T(8,128)(2,1)S(1)} copy-done((bf16[128,1024]{1,0:T(8,128)(2,1)S(1)}, bf16[128,1024]{1,0:T(8,128)(2,1)}, u32[]{:S(2)}) %copy-start) | copy-done | bytes 262168
  1.6 91.4 %shard_map.37 = f32[256,256]{1,0:T(8,128)S(1)} custom-call(bf16[128,1024]{1,0:T(8,128)(2,1)S(1)} %copy-done, s32[64]{0:T(128)S(1)} %copy-done.1, s32[1]{0:T(128)S(6)} %copy.5.start_hbm), custom_call_target="tpu_custom_call" | custom-call | tf_op jit(solution)/shard_map/pallas_call | solution.py:367
  93.1 0.7 copy.6
Async XLA Ops:
  0.0 0.7 copy-start.1
  0.7 1.0 %copy-start = (bf16[128,1024]{1,0:T(8,128)(2,1)S(1)}, bf16[128,1024]{1,0:T(8,128)(2,1)}, u32[]{:S(2)}) copy-start(bf16[128,1024]{1,0:T(8,128)(2,1)} %density_ref.1) | copy-start | bytes 786436
